TPU v7x, 128 devices: a whole 4x4x4 slice. The times are simulated.
128 devices in a mesh: blk: 64 (over y, x_lo, z, core), tower: 2 (over x_hi).
Axes of the slice: x: 4 (x_hi: 2, x_lo: 2; x = x_hi * 2 + x_lo), y: 4, z: 4, core: 2. Of those that a mesh axis runs over, the one named last changes fastest.
Arguments:
- vision_features: bfloat16 [65536, 1152], P('blk', 'tower'), may hold values from -36 to 36
- caption_features: bfloat16 [65536, 1152], P('blk', 'tower'), may hold values from -36 to 36
- sample_importance: bfloat16 [65536], P('blk'), may hold values from 0.5 to 18, as said below
- scale_exponent: float32 [1], replicated, may hold values from 2.3 to 3.4
- similarity_shift: float32 [1], replicated, may hold values from -3 to -1
Outputs:
- image_gradient: bfloat16 [65536, 1152], P('blk', 'tower')
- text_gradient: bfloat16 [65536, 1152], P('blk', 'tower')
- scalars: float32 [3], replicated
Inputs may be any that keep to these rules, and one draw needn't show every extreme that they name: `sample_importance`: positive loss weight of each pair.
All inputs are finite; a program needn't handle non-finite values.
Results may differ from a plain program's by a relative error of at most 0.012.
Values may be sent and summed in bfloat16 or wider, within the bound.
A program may use at most 64 MiB of HBM per device.

v0:
```python
import functools
import math

import jax
import jax.numpy as jnp
from jax import lax
from jax.experimental import pallas as pl
from jax.experimental.pallas import tpu as pltpu
from jax.sharding import PartitionSpec as P

MESH = pl.DeviceIdType.MESH
F32, BF16 = jnp.float32, jnp.bfloat16
TXT, IMG = 0, 1
BLOCK = 512
SUPER = 1024
PART = 576
FULL = 1152
CHUNK = 256
CHUNKS = SUPER // CHUNK
AHEAD = 3
PIECES = 4
LINE = 8
LOG2E = math.log2(math.e)


def fold(v):
    total = v[:, :128]
    for k in range(1, v.shape[1] // 128):
        total = total + v[:, 128 * k : 128 * (k + 1)]
    return total


def row_of(partial):
    return jnp.sum(jnp.transpose(partial), axis=0, keepdims=True)


def kernel(
    count,
    txt_in,
    img_in,
    weight_in,
    exponent,
    offset,
    img_out,
    txt_out,
    sums_out,
    held,
    weights,
    inv_row,
    inv_col,
    turned_txt,
    turned_img,
    txt_grad,
    txt_along,
    tallies,
    staged,
    coef,
    line_sums,
    all_sums,
    load_sem,
    x_send,
    x_recv,
    own_send,
    own_recv,
    other_send,
    other_recv,
    weight_send,
    weight_recv,
    out_sem,
    line_send,
    line_recv,
    all_send,
    all_recv,
):
    sb = lax.axis_index("blk")
    tower = lax.axis_index("tower")
    away = 1 - tower
    left, right = lax.rem(sb + count - 1, count), lax.rem(sb + 1, count)
    place, line = lax.rem(sb, LINE), sb // LINE
    lines = count // LINE
    rank = place * 2 + tower
    left_end, right_end = place == 0, place == LINE - 1
    inputs = (txt_in, img_in)
    sides = ((0, left, left_end), (1, right, right_end))

    def line_peer(k):
        there = lax.rem(rank + k, 2 * LINE)
        return there, (line * LINE + there // 2, lax.rem(there, 2))

    def all_peer(k):
        there = lax.rem(line + k, lines)
        return there, (there * LINE + place, tower)

    def columns_of(slot, c):
        return pl.ds(pl.multiple_of(slot * SUPER + c * CHUNK, CHUNK), CHUNK)

    def whole(slot):
        return pl.ds(slot * SUPER, SUPER)

    loads = []
    for a in range(2):
        target = held.at[a, pl.ds(0, PART), whole(1)]
        loads.append(pltpu.make_async_copy(inputs[a], target, load_sem.at[a]))
        loads[a].start()

    barrier = pltpu.get_barrier_semaphore()

    def greet(where):
        pl.semaphore_signal(barrier, inc=1, device_id=where, device_id_type=MESH)

    for where in ((sb, away), (left, tower), (right, tower)):
        greet(where)

    @pl.when(left_end)
    def _():
        greet((left, away))

    @pl.when(right_end)
    def _():
        greet((right, away))

    def greet_line(k, carry):
        greet(line_peer(k)[1])
        return carry

    def greet_all(k, carry):
        greet(all_peer(k)[1])
        return carry

    lax.fori_loop(1, 2 * LINE, greet_line, 0)
    lax.fori_loop(1, lines, greet_all, 0)
    at_end = jnp.logical_or(left_end, right_end)
    pl.semaphore_wait(barrier, jnp.where(at_end, 4, 3) + (2 * LINE - 1) + (lines - 1))

    def x_copy(a, c):
        return pltpu.make_async_remote_copy(
            src_ref=inputs[a].at[:, pl.ds(c * CHUNK, CHUNK)],
            dst_ref=held.at[a, pl.ds(PART, PART), columns_of(1, c)],
            send_sem=x_send.at[a, c],
            recv_sem=x_recv.at[a, c],
            device_id=(sb, away),
            device_id_type=MESH,
        )

    def own_copy(a, side, c):
        n, where, _ = sides[side]
        return pltpu.make_async_remote_copy(
            src_ref=inputs[a].at[:, pl.ds(c * CHUNK, CHUNK)],
            dst_ref=held.at[a, pl.ds(0, PART), columns_of(2 - 2 * n, c)],
            send_sem=own_send.at[a, n, c],
            recv_sem=own_recv.at[a, n, c],
            device_id=(where, tower),
            device_id_type=MESH,
        )

    def other_copy(a, side, c, cross=False):
        n, where, _ = sides[side]
        here = pl.ds(c * CHUNK, CHUNK)
        return pltpu.make_async_remote_copy(
            src_ref=inputs[a].at[:, here] if cross else held.at[a, pl.ds(PART, PART), columns_of(1, c)],
            dst_ref=held.at[a, pl.ds(PART, PART), columns_of(2 - 2 * n, c)],
            send_sem=other_send.at[a, n, c],
            recv_sem=other_recv.at[a, n, c],
            device_id=(where, away if cross else tower),
            device_id_type=MESH,
        )

    def begin(a, c):
        x_copy(a, c).start()
        for side in range(2):
            own_copy(a, side, c).start()

            @pl.when(sides[side][2])
            def _():
                other_copy(a, side, c, cross=True).start()

    def weight_copy(side):
        n, where, _ = sides[side]
        return pltpu.make_async_remote_copy(
            src_ref=weights.at[1],
            dst_ref=weights.at[2 - 2 * n],
            send_sem=weight_send.at[n],
            recv_sem=weight_recv.at[n],
            device_id=(where, tower),
            device_id_type=MESH,
        )

    def line_copy(k, source):
        there, where = line_peer(k)
        return pltpu.make_async_remote_copy(
            src_ref=tallies,
            dst_ref=line_sums.at[source],
            send_sem=line_send.at[k],
            recv_sem=line_recv.at[source],
            device_id=where,
            device_id_type=MESH,
        )

    def all_copy(k, source):
        there, where = all_peer(k)
        return pltpu.make_async_remote_copy(
            src_ref=tallies,
            dst_ref=all_sums.at[source],
            send_sem=all_send.at[k],
            recv_sem=all_recv.at[source],
            device_id=where,
            device_id_type=MESH,
        )

    for c in range(AHEAD):
        begin(TXT, c)
    heavy = weight_in[...].astype(F32)
    for k in range(8):
        weights[1, :, 128 * k : 128 * (k + 1)] = jnp.broadcast_to(heavy[k : k + 1], (8, 128))
    for side in range(2):
        weight_copy(side).start()

    scale = jnp.exp(jnp.full((1, 128), exponent[0], F32))[:, 0:1]
    scale2 = scale * LOG2E
    shift2 = offset[0] * LOG2E

    txt_grad[...] = jnp.zeros_like(txt_grad)
    txt_along[...] = jnp.zeros_like(txt_along)
    tallies[...] = jnp.zeros_like(tallies)
    for load in loads:
        load.wait()

    def norms(a, slot, c):
        wide = held[a, :, columns_of(slot, c)].astype(F32)
        total = jnp.sum(wide * wide, axis=0, keepdims=True)
        inverse = lax.rsqrt(total + 1e-06)
        here = pl.ds(pl.multiple_of(c * CHUNK, CHUNK), CHUNK)
        inv_row[a, slot, :, here] = jnp.broadcast_to(inverse, (8, CHUNK))
        if slot == 1:
            inv_col[a, here, :] = jnp.transpose(jnp.broadcast_to(inverse, (128, CHUNK)))

    def forward(a, c):
        @pl.when(c < CHUNKS - AHEAD)
        def _():
            begin(a, c + AHEAD)

        if a == TXT:

            @pl.when(c >= CHUNKS - AHEAD)
            def _():
                begin(IMG, c - (CHUNKS - AHEAD))

        x_copy(a, c).wait_recv()
        for side in range(2):
            pl.when(jnp.logical_not(sides[side][2]))(other_copy(a, side, c).start)

    def from_sides(a, c):
        for side in range(2):
            own_copy(a, 1 - side, c).wait_recv()
            other_copy(a, 1 - side, c).wait_recv()
            norms(a, 2 * side, c)

    def text_step(c, carry):
        forward(TXT, c)
        norms(TXT, 1, c)
        here = pl.ds(pl.multiple_of(c * CHUNK, CHUNK), CHUNK)
        turned_txt[here, :] = jnp.transpose(held[TXT, :, columns_of(1, c)])

        @pl.when(c > 0)
        def _():
            from_sides(TXT, c - 1)

        return carry

    lax.fori_loop(0, CHUNKS, text_step, 0)
    for side in range(2):
        weight_copy(1 - side).wait_recv()

    def image_out_copy(c):
        here = pl.ds(pl.multiple_of(c * CHUNK, CHUNK), CHUNK)
        return pltpu.make_async_copy(staged.at[IMG, :, here], img_out.at[:, here], out_sem.at[c])

    def image_product(c, j):
        first = pl.multiple_of((c // 2 + j) * BLOCK, BLOCK)
        return jnp.dot(
            turned_img[...], held[TXT, :, pl.ds(first, BLOCK)], preferred_element_type=F32
        )

    def image_coef(c, j, product, sums):
        along, bias, loss = sums
        here = pl.ds(pl.multiple_of(c * CHUNK, CHUNK), CHUNK)
        row_scale = inv_col[IMG, here, 0:1] * scale2
        first = pl.multiple_of((c // 2 + j) * BLOCK, BLOCK)
        slot, inside = first // SUPER, lax.rem(first, SUPER)
        inv_text = inv_row[TXT, slot, 0:1, pl.ds(pl.multiple_of(inside, BLOCK), BLOCK)]
        logits2 = product * inv_text * row_scale + shift2
        grown = jnp.exp2(logits2)
        more = grown + 1.0
        sig = grown / more
        loss = loss + fold(jnp.log(more[:, :CHUNK] * more[:, CHUNK:]))
        if j == 2:
            mine = lax.broadcasted_iota(jnp.int32, (CHUNK, BLOCK), 0) + lax.rem(c, 2) * CHUNK
            match = mine == lax.broadcasted_iota(jnp.int32, (CHUNK, BLOCK), 1)
            sig = jnp.where(match, sig - 1.0, sig)
            loss = loss - fold(jnp.where(match, logits2, 0.0)) * (1.0 / LOG2E)
        scaled = sig * inv_text
        along = along + fold(scaled * product)
        bias = bias + fold(sig)
        coef[:, pl.ds(j * BLOCK, BLOCK)] = scaled.astype(BF16)
        return along, bias, loss

    def image_grad(c, sums):
        along, bias, loss = sums
        here = pl.ds(pl.multiple_of(c * CHUNK, CHUNK), CHUNK)
        band = pl.ds(pl.multiple_of(c // 2 * BLOCK, BLOCK), 5 * BLOCK)
        grad = lax.dot_general(
            held[TXT, pl.ds(0, PART), band],
            coef[...],
            (((1,), (1,)), ((), ())),
            preferred_element_type=F32,
        )
        weight = weights[1, 0:1, here]
        inverse = inv_row[IMG, 1, 0:1, here]
        along_row = row_of(along) * inverse
        wide = held[IMG, pl.ds(0, PART), columns_of(1, c)].astype(F32)
        result = (weight * inverse * scale) * (grad - wide * (inverse * along_row))
        staged[IMG, :, here] = result.astype(BF16)
        image_out_copy(c).start()
        for n, value in enumerate((row_of(loss), scale * along_row, row_of(bias))):
            total = jnp.sum(weight * value, axis=1, keepdims=True)
            tallies[n : n + 1, :] += jnp.broadcast_to(total, (1, 128))

    def text_product(slot, c, block):
        rows = pl.ds(pl.multiple_of(block * BLOCK, BLOCK), BLOCK)
        return jnp.dot(
            turned_txt[rows, :], held[IMG, :, columns_of(slot, c)], preferred_element_type=F32
        )

    def text_coef(slot, c, block, product, diagonal):
        rows = pl.ds(pl.multiple_of(block * BLOCK, BLOCK), BLOCK)
        here = pl.ds(pl.multiple_of(c * CHUNK, CHUNK), CHUNK)
        inv_image = inv_row[IMG, slot, 0:1, here]
        heavy = inv_image * weights[slot, 0:1, here]
        row_scale = inv_col[TXT, rows, 0:1] * scale2
        grown = jnp.exp2(product * inv_image * row_scale + shift2)
        sig = grown / (grown + 1.0)
        if diagonal:
            mine = lax.broadcasted_iota(jnp.int32, (BLOCK, CHUNK), 0) + block * BLOCK
            other = lax.broadcasted_iota(jnp.int32, (BLOCK, CHUNK), 1) + c * CHUNK
            sig = jnp.where(mine == other, sig - 1.0, sig)
        scaled = sig * heavy
        txt_along[rows, :] += fold(scaled * product)
        return scaled.astype(BF16)

    def text_grad(slot, c, block, scaled):
        rows = pl.ds(pl.multiple_of(block * BLOCK, BLOCK), BLOCK)
        txt_grad[:, rows] += lax.dot_general(
            held[IMG, pl.ds(0, PART), columns_of(slot, c)],
            scaled,
            (((1,), (1,)), ((), ())),
            preferred_element_type=F32,
        )

    def own_pairs(c):
        turned_img[...] = jnp.transpose(held[IMG, :, columns_of(1, c)])
        zero = jnp.zeros((CHUNK, 128), F32)
        sums = (zero, zero, zero)
        product = image_product(c, 0)
        for j in range(5):
            after = image_product(c, j + 1) if j < 4 else text_product(1, c, 0)
            sums = image_coef(c, j, product, sums)
            product = after
        after = text_product(1, c, 1)
        image_grad(c, sums)
        scaled = text_coef(1, c, 0, product, True)
        text_grad(1, c, 0, scaled)
        scaled = text_coef(1, c, 1, after, True)
        text_grad(1, c, 1, scaled)

    def side_pairs(c):
        late = c >= CHUNKS // 2
        jobs = [(0, 0), (2, 1), (jnp.where(late, 0, 2), jnp.where(late, 1, 0))]
        product = text_product(jobs[0][0], c, jobs[0][1])
        for n, (slot, block) in enumerate(jobs):
            after = text_product(jobs[n + 1][0], c, jobs[n + 1][1]) if n < 2 else None
            scaled = text_coef(slot, c, block, product, False)
            text_grad(slot, c, block, scaled)
            product = after

    def image_step(c, carry):
        forward(IMG, c)
        norms(IMG, 1, c)

        @pl.when(c == 0)
        def _():
            from_sides(TXT, CHUNKS - 1)

        own_pairs(c)

        @pl.when(c == CHUNKS - 1)
        def _():
            def send(k, carry):
                line_copy(k, rank).start()
                return carry

            lax.fori_loop(1, 2 * LINE, send, 0)

        from_sides(IMG, c)
        side_pairs(c)
        return carry

    lax.fori_loop(0, CHUNKS, image_step, 0)

    def line_wait(k, carry):
        copy = line_copy(k, line_peer(k)[0])
        copy.wait_recv()
        copy.wait_send()
        return carry

    line_sums[rank] = tallies[...]
    lax.fori_loop(1, 2 * LINE, line_wait, 0)
    total = line_sums[0]
    for k in range(1, 2 * LINE):
        total = total + line_sums[k]
    tallies[...] = total
    all_sums[line] = total

    def all_send_one(k, carry):
        all_copy(k, line).start()
        return carry

    lax.fori_loop(1, lines, all_send_one, 0)

    def text_out_copy(c):
        here = pl.ds(c * CHUNK, CHUNK)
        return pltpu.make_async_copy(
            staged.at[TXT, :, here], txt_out.at[:, here], out_sem.at[CHUNKS + c]
        )

    for c in range(CHUNKS):
        here = pl.ds(c * CHUNK, CHUNK)
        inverse = inv_row[TXT, 1, 0:1, here]
        along_row = row_of(txt_along[here, :]) * inverse
        wide = held[TXT, pl.ds(0, PART), columns_of(1, c)].astype(F32)
        result = (inverse * scale) * (txt_grad[:, here] - wide * (inverse * along_row))
        staged[TXT, :, here] = result.astype(BF16)
        text_out_copy(c).start()

    def all_wait(k, carry):
        copy = all_copy(k, all_peer(k)[0])
        copy.wait_recv()
        copy.wait_send()
        return carry

    lax.fori_loop(1, lines, all_wait, 0)
    total = all_sums[0]
    for k in range(1, lines):
        total = total + all_sums[k]
    sums_out[...] = total * (1.0 / (2.0 * count * SUPER * 5 * BLOCK))

    for c in range(CHUNKS):
        image_out_copy(c).wait()
        text_out_copy(c).wait()
    for a in range(2):
        for c in range(CHUNKS):
            x_copy(a, c).wait_send()
            for side in range(2):
                own_copy(a, side, c).wait_send()
                other_copy(a, side, c).wait_send()
    for side in range(2):
        weight_copy(side).wait_send()


def deliver(img_in, txt_in, sums, img_out, txt_out, scalars, held, load_sem, store_sem):
    loads, stores = [], []
    for a, (source, target) in enumerate(((img_in, img_out), (txt_in, txt_out))):
        for k in range(PIECES):
            rows = pl.ds(k * PART // PIECES, PART // PIECES)
            loads.append(pltpu.make_async_copy(source.at[rows], held.at[a, rows], load_sem.at[a, k]))
            stores.append(pltpu.make_async_copy(held.at[a, rows], target.at[rows], store_sem.at[a, k]))
            loads[-1].start()
    for n in range(3):
        scalars[n] = sums[n, 0]
    for load, store in zip(loads, stores):
        load.wait()
        store.start()
    for store in stores:
        store.wait()


def shards(count, vision, caption, importance, scale_exponent, similarity_shift):
    lines = count // LINE
    dma = pltpu.SemaphoreType.DMA
    hbm, vmem = pl.BlockSpec(memory_space=pl.ANY), pl.BlockSpec(memory_space=pltpu.VMEM)
    smem = pl.BlockSpec(memory_space=pltpu.SMEM)
    img_out, txt_out, sums = pl.pallas_call(
        functools.partial(kernel, count),
        out_shape=(
            jax.ShapeDtypeStruct((PART, SUPER), BF16),
            jax.ShapeDtypeStruct((PART, SUPER), BF16),
            jax.ShapeDtypeStruct((8, 128), F32),
        ),
        in_specs=[hbm, hbm, vmem, smem, smem],
        out_specs=(hbm, hbm, vmem),
        scratch_shapes=[
            pltpu.VMEM((2, FULL, 3 * SUPER), BF16),
            pltpu.VMEM((3, 8, SUPER), F32),
            pltpu.VMEM((2, 3, 8, SUPER), F32),
            pltpu.VMEM((2, SUPER, 128), F32),
            pltpu.VMEM((SUPER, FULL), BF16),
            pltpu.VMEM((CHUNK, FULL), BF16),
            pltpu.VMEM((PART, SUPER), F32),
            pltpu.VMEM((SUPER, 128), F32),
            pltpu.VMEM((8, 128), F32),
            pltpu.VMEM((2, PART, SUPER), BF16),
            pltpu.VMEM((CHUNK, 5 * BLOCK), BF16),
            pltpu.VMEM((2 * LINE, 8, 128), F32),
            pltpu.VMEM((lines, 8, 128), F32),
            dma((2,)),
            dma((2, CHUNKS)),
            dma((2, CHUNKS)),
            dma((2, 2, CHUNKS)),
            dma((2, 2, CHUNKS)),
            dma((2, 2, CHUNKS)),
            dma((2, 2, CHUNKS)),
            dma((2,)),
            dma((2,)),
            dma((2 * CHUNKS,)),
            dma((2 * LINE,)),
            dma((2 * LINE,)),
            dma((lines,)),
            dma((lines,)),
        ],
        compiler_params=pltpu.CompilerParams(
            collective_id=0, has_side_effects=True, vmem_limit_bytes=60 * 2**20
        ),
        name="band",
    )(caption.T, vision.T, importance.reshape(8, SUPER // 8), scale_exponent, similarity_shift)
    img_out, txt_out, scalars = pl.pallas_call(
        deliver,
        out_shape=(
            jax.ShapeDtypeStruct((PART, SUPER), BF16),
            jax.ShapeDtypeStruct((PART, SUPER), BF16),
            jax.ShapeDtypeStruct((3,), F32),
        ),
        in_specs=[hbm, hbm, smem],
        out_specs=(hbm, hbm, smem),
        scratch_shapes=[pltpu.VMEM((2, PART, SUPER), BF16), dma((2, PIECES)), dma((2, PIECES))],
        name="deliver",
    )(img_out, txt_out, sums)
    return img_out.T, txt_out.T, scalars


def solution(mesh):
    in_specs = (P("blk", "tower"), P("blk", "tower"), P("blk"), P(), P())
    out_specs = (P("blk", "tower"), P("blk", "tower"), P())
    return jax.shard_map(
        functools.partial(shards, mesh.shape["blk"]),
        mesh=mesh,
        in_specs=in_specs,
        out_specs=out_specs,
        check_vma=False,
    )
```

profile of v0, /device:TPU:0, one launch (start us, length us, event | category | flops | bytes accessed | tf_op | source)
XLA Modules:
  0.0 112.0 jit_solution(3999576934484140432)
XLA Ops:
  1.9 106.3 %band.1 = (bf16[576,1024]{1,0:T(8,128)(2,1)}, bf16[576,1024]{1,0:T(8,128)(2,1)}, f32[8,128]{1,0:T(8,128)}) custom-call(bf16[576,1024]{1,0:T(8,128)(2,1)} %bitcast.5, bf16[576,1024]{1,0:T(8,128)(2,1)} %bitcast.6, bf16[8,128]{1,0:T(8,128)(2,1)} %bitcast.7, f32[1]{0:T(128)S(6)} %copy.8.exponent, f32[1]{0:T(128)S(6)} %copy.9.offset), custom_call_target="tpu_custom_call" | custom-call | tf_op jit(solution)/shard_map/band/pallas_call | solution.py:491
  108.3 3.7 %deliver.1 = (bf16[576,1024]{1,0:T(8,128)(2,1)}, bf16[576,1024]{1,0:T(8,128)(2,1)}, f32[3]{0:T(128)}) custom-call(bf16[576,1024]{1,0:T(8,128)(2,1)} %get-tuple-element.9.img_in, bf16[576,1024]{1,0:T(8,128)(2,1)} %get-tuple-element.10.txt_in, f32[8,128]{1,0:T(8,128)} %get-tuple-element.11.sums), custom_call_target="tpu_custom_call" | custom-call | tf_op jit(solution)/shard_map/deliver/pallas_call | solution.py:534
where the time goes:
time: 112 us
  Pallas kernels  110 us (98%)
  between operations  1.93 us (2%)
    pallas_call x1, Pallas kernels, shards(): pl.pallas_call(functools.partial(kernel, count), out_shape=(jax.ShapeDtyp...  106 us
    pallas_call x1, Pallas kernels, shards(): pl.pallas_call(deliver, out_shape=(jax.ShapeDtypeStruct((PART, SUPER), BF...  3.73 us

commit v1 on v0

--- a/solution.py
+++ b/solution.py
@@ -17,8 +17,7 @@
 FULL = 1152
 CHUNK = 256
 CHUNKS = SUPER // CHUNK
-AHEAD = 3
-PIECES = 4
+AHEAD = 1
 LINE = 8
 LOG2E = math.log2(math.e)
 
@@ -53,9 +52,9 @@
     txt_grad,
     txt_along,
     tallies,
-    staged,
     coef,
     line_sums,
+    line_out,
     all_sums,
     load_sem,
     x_send,
@@ -66,7 +65,6 @@
     other_recv,
     weight_send,
     weight_recv,
-    out_sem,
     line_send,
     line_recv,
     all_send,
@@ -199,7 +197,7 @@
     def all_copy(k, source):
         there, where = all_peer(k)
         return pltpu.make_async_remote_copy(
-            src_ref=tallies,
+            src_ref=line_out,
             dst_ref=all_sums.at[source],
             send_sem=all_send.at[k],
             recv_sem=all_recv.at[source],
@@ -270,10 +268,6 @@
     lax.fori_loop(0, CHUNKS, text_step, 0)
     for side in range(2):
         weight_copy(1 - side).wait_recv()
-
-    def image_out_copy(c):
-        here = pl.ds(pl.multiple_of(c * CHUNK, CHUNK), CHUNK)
-        return pltpu.make_async_copy(staged.at[IMG, :, here], img_out.at[:, here], out_sem.at[c])
 
     def image_product(c, j):
         first = pl.multiple_of((c // 2 + j) * BLOCK, BLOCK)
@@ -319,8 +313,7 @@
         along_row = row_of(along) * inverse
         wide = held[IMG, pl.ds(0, PART), columns_of(1, c)].astype(F32)
         result = (weight * inverse * scale) * (grad - wide * (inverse * along_row))
-        staged[IMG, :, here] = result.astype(BF16)
-        image_out_copy(c).start()
+        img_out[:, here] = result.astype(BF16)
         for n, value in enumerate((row_of(loss), scale * along_row, row_of(bias))):
             total = jnp.sum(weight * value, axis=1, keepdims=True)
             tallies[n : n + 1, :] += jnp.broadcast_to(total, (1, 128))
@@ -362,11 +355,18 @@
         sums = (zero, zero, zero)
         product = image_product(c, 0)
         for j in range(5):
-            after = image_product(c, j + 1) if j < 4 else text_product(1, c, 0)
+            after = image_product(c, j + 1) if j < 4 else None
             sums = image_coef(c, j, product, sums)
             product = after
+        image_grad(c, sums)
+
+        @pl.when(c == CHUNKS - 1)
+        def _():
+            for k in range(1, 2 * LINE):
+                line_copy(k, rank).start()
+
+        product = text_product(1, c, 0)
         after = text_product(1, c, 1)
-        image_grad(c, sums)
         scaled = text_coef(1, c, 0, product, True)
         text_grad(1, c, 0, scaled)
         scaled = text_coef(1, c, 1, after, True)
@@ -382,6 +382,18 @@
             text_grad(slot, c, block, scaled)
             product = after
 
+    def line_total():
+        line_sums[rank] = tallies[...]
+        for k in range(1, 2 * LINE):
+            line_copy(k, line_peer(k)[0]).wait_recv()
+        total = line_sums[0]
+        for k in range(1, 2 * LINE):
+            total = total + line_sums[k]
+        line_out[...] = total
+        all_sums[line] = total
+        for k in range(1, lines):
+            all_copy(k, line).start()
+
     def image_step(c, carry):
         forward(IMG, c)
         norms(IMG, 1, c)
@@ -392,45 +404,12 @@
 
         own_pairs(c)
 
-        @pl.when(c == CHUNKS - 1)
-        def _():
-            def send(k, carry):
-                line_copy(k, rank).start()
-                return carry
-
-            lax.fori_loop(1, 2 * LINE, send, 0)
-
+        pl.when(c == CHUNKS - 1)(line_total)
         from_sides(IMG, c)
         side_pairs(c)
         return carry
 
     lax.fori_loop(0, CHUNKS, image_step, 0)
-
-    def line_wait(k, carry):
-        copy = line_copy(k, line_peer(k)[0])
-        copy.wait_recv()
-        copy.wait_send()
-        return carry
-
-    line_sums[rank] = tallies[...]
-    lax.fori_loop(1, 2 * LINE, line_wait, 0)
-    total = line_sums[0]
-    for k in range(1, 2 * LINE):
-        total = total + line_sums[k]
-    tallies[...] = total
-    all_sums[line] = total
-
-    def all_send_one(k, carry):
-        all_copy(k, line).start()
-        return carry
-
-    lax.fori_loop(1, lines, all_send_one, 0)
-
-    def text_out_copy(c):
-        here = pl.ds(c * CHUNK, CHUNK)
-        return pltpu.make_async_copy(
-            staged.at[TXT, :, here], txt_out.at[:, here], out_sem.at[CHUNKS + c]
-        )
 
     for c in range(CHUNKS):
         here = pl.ds(c * CHUNK, CHUNK)
@@ -438,24 +417,17 @@
         along_row = row_of(txt_along[here, :]) * inverse
         wide = held[TXT, pl.ds(0, PART), columns_of(1, c)].astype(F32)
         result = (inverse * scale) * (txt_grad[:, here] - wide * (inverse * along_row))
-        staged[TXT, :, here] = result.astype(BF16)
-        text_out_copy(c).start()
-
-    def all_wait(k, carry):
-        copy = all_copy(k, all_peer(k)[0])
-        copy.wait_recv()
-        copy.wait_send()
-        return carry
-
-    lax.fori_loop(1, lines, all_wait, 0)
+        txt_out[:, here] = result.astype(BF16)
+
+    for k in range(1, lines):
+        all_copy(k, all_peer(k)[0]).wait_recv()
     total = all_sums[0]
     for k in range(1, lines):
         total = total + all_sums[k]
-    sums_out[...] = total * (1.0 / (2.0 * count * SUPER * 5 * BLOCK))
-
-    for c in range(CHUNKS):
-        image_out_copy(c).wait()
-        text_out_copy(c).wait()
+    total = total * (1.0 / (2.0 * count * SUPER * 5 * BLOCK))
+    for n in range(3):
+        sums_out[n] = jnp.max(total[n : n + 1, :])
+
     for a in range(2):
         for c in range(CHUNKS):
             x_copy(a, c).wait_send()
@@ -464,23 +436,10 @@
                 other_copy(a, side, c).wait_send()
     for side in range(2):
         weight_copy(side).wait_send()
-
-
-def deliver(img_in, txt_in, sums, img_out, txt_out, scalars, held, load_sem, store_sem):
-    loads, stores = [], []
-    for a, (source, target) in enumerate(((img_in, img_out), (txt_in, txt_out))):
-        for k in range(PIECES):
-            rows = pl.ds(k * PART // PIECES, PART // PIECES)
-            loads.append(pltpu.make_async_copy(source.at[rows], held.at[a, rows], load_sem.at[a, k]))
-            stores.append(pltpu.make_async_copy(held.at[a, rows], target.at[rows], store_sem.at[a, k]))
-            loads[-1].start()
-    for n in range(3):
-        scalars[n] = sums[n, 0]
-    for load, store in zip(loads, stores):
-        load.wait()
-        store.start()
-    for store in stores:
-        store.wait()
+    for k in range(1, 2 * LINE):
+        line_copy(k, rank).wait_send()
+    for k in range(1, lines):
+        all_copy(k, line).wait_send()
 
 
 def shards(count, vision, caption, importance, scale_exponent, similarity_shift):
@@ -491,12 +450,12 @@
     img_out, txt_out, sums = pl.pallas_call(
         functools.partial(kernel, count),
         out_shape=(
-            jax.ShapeDtypeStruct((PART, SUPER), BF16),
-            jax.ShapeDtypeStruct((PART, SUPER), BF16),
-            jax.ShapeDtypeStruct((8, 128), F32),
+            pltpu.VMEM((PART, SUPER), BF16),
+            pltpu.VMEM((PART, SUPER), BF16),
+            jax.ShapeDtypeStruct((3,), F32),
         ),
         in_specs=[hbm, hbm, vmem, smem, smem],
-        out_specs=(hbm, hbm, vmem),
+        out_specs=(vmem, vmem, smem),
         scratch_shapes=[
             pltpu.VMEM((2, FULL, 3 * SUPER), BF16),
             pltpu.VMEM((3, 8, SUPER), F32),
@@ -507,9 +466,9 @@
             pltpu.VMEM((PART, SUPER), F32),
             pltpu.VMEM((SUPER, 128), F32),
             pltpu.VMEM((8, 128), F32),
-            pltpu.VMEM((2, PART, SUPER), BF16),
             pltpu.VMEM((CHUNK, 5 * BLOCK), BF16),
             pltpu.VMEM((2 * LINE, 8, 128), F32),
+            pltpu.VMEM((8, 128), F32),
             pltpu.VMEM((lines, 8, 128), F32),
             dma((2,)),
             dma((2, CHUNKS)),
@@ -520,7 +479,6 @@
             dma((2, 2, CHUNKS)),
             dma((2,)),
             dma((2,)),
-            dma((2 * CHUNKS,)),
             dma((2 * LINE,)),
             dma((2 * LINE,)),
             dma((lines,)),
@@ -531,19 +489,7 @@
         ),
         name="band",
     )(caption.T, vision.T, importance.reshape(8, SUPER // 8), scale_exponent, similarity_shift)
-    img_out, txt_out, scalars = pl.pallas_call(
-        deliver,
-        out_shape=(
-            jax.ShapeDtypeStruct((PART, SUPER), BF16),
-            jax.ShapeDtypeStruct((PART, SUPER), BF16),
-            jax.ShapeDtypeStruct((3,), F32),
-        ),
-        in_specs=[hbm, hbm, smem],
-        out_specs=(hbm, hbm, smem),
-        scratch_shapes=[pltpu.VMEM((2, PART, SUPER), BF16), dma((2, PIECES)), dma((2, PIECES))],
-        name="deliver",
-    )(img_out, txt_out, sums)
-    return img_out.T, txt_out.T, scalars
+    return img_out.T, txt_out.T, sums
 
 
 def solution(mesh):

time: 112 us -> 110 us (0.982)
  Pallas kernels: 110 us -> 106 us
  local copies, waits for them, and re-layouts: 0 us -> 2.54 us
    pallas_call x2 -> x1, Pallas kernels: 110 us -> 106 us  [shards(): pl.pallas_call(functools.partial(kernel, count), out_shape=(pltpu.VMEM((P...]
    unnamed x0 -> x5, local copies, waits for them, and re-layouts: none -> 2.54 us
where the time goes in v1:
time: 110 us
  Pallas kernels  106 us (96%)
  local copies, waits for them, and re-layouts  2.54 us (2%)
  between operations  1.93 us (2%)
    pallas_call x1, Pallas kernels, shards(): pl.pallas_call(functools.partial(kernel, count), out_shape=(pltpu.VMEM((P...  106 us
    unnamed x5, local copies, waits for them, and re-layouts  2.54 us

profile of v1, /device:TPU:0, one launch (start us, length us, event | category | flops | bytes accessed | tf_op | source)
XLA Modules:
  0.0 110.2 jit_solution(18141151749111403003)
XLA Ops:
  1.9 105.8 %band.1 = (bf16[576,1024]{1,0:T(8,128)(2,1)S(1)}, bf16[576,1024]{1,0:T(8,128)(2,1)S(1)}, f32[3]{0:T(128)}) custom-call(bf16[576,1024]{1,0:T(8,128)(2,1)} %bitcast.7, bf16[576,1024]{1,0:T(8,128)(2,1)} %bitcast.8, bf16[8,128]{1,0:T(8,128)(2,1)} %bitcast.9, f32[1]{0:T(128)S(6)} %copy.13.exponent, f32[1]{0:T(128)S(6)} %copy.14.offset), custom_call_target="tpu_custom_call" | custom-call | tf_op jit(solution)/shard_map/band/pallas_call | solution.py:450
  107.7 1.0 copy.11
  108.7 0.0 copy-start
  108.7 1.0 copy.12
  109.7 0.0 copy-done
  109.7 0.5 copy.15
Async XLA Ops:
  108.7 1.0 copy-start

commit v2 on v1

--- a/solution.py
+++ b/solution.py
@@ -165,6 +165,8 @@
 
     def begin(a, c):
         x_copy(a, c).start()
+
+    def begin_sides(a, c):
         for side in range(2):
             own_copy(a, side, c).start()
 
@@ -207,6 +209,7 @@
 
     for c in range(AHEAD):
         begin(TXT, c)
+        begin_sides(TXT, c)
     heavy = weight_in[...].astype(F32)
     for k in range(8):
         weights[1, :, 128 * k : 128 * (k + 1)] = jnp.broadcast_to(heavy[k : k + 1], (8, 128))
@@ -232,20 +235,23 @@
         if slot == 1:
             inv_col[a, here, :] = jnp.transpose(jnp.broadcast_to(inverse, (128, CHUNK)))
 
-    def forward(a, c):
+    def ahead(a, c, start):
         @pl.when(c < CHUNKS - AHEAD)
         def _():
-            begin(a, c + AHEAD)
+            start(a, c + AHEAD)
 
         if a == TXT:
 
             @pl.when(c >= CHUNKS - AHEAD)
             def _():
-                begin(IMG, c - (CHUNKS - AHEAD))
-
+                start(IMG, c - (CHUNKS - AHEAD))
+
+    def forward(a, c):
+        ahead(a, c, begin)
         x_copy(a, c).wait_recv()
         for side in range(2):
             pl.when(jnp.logical_not(sides[side][2]))(other_copy(a, side, c).start)
+        ahead(a, c, begin_sides)
 
     def from_sides(a, c):
         for side in range(2):

time: 110 us -> 110 us (level)
  no operation moved by 1% of the time
where the time goes in v2:
time: 110 us
  Pallas kernels  105 us (95%)
  local copies, waits for them, and re-layouts  2.54 us (2%)
  between operations  1.93 us (2%)
    pallas_call x1, Pallas kernels, shards(): pl.pallas_call(functools.partial(kernel, count), out_shape=(pltpu.VMEM((P...  105 us
    unnamed x5, local copies, waits for them, and re-layouts  2.54 us

profile of v2, /device:TPU:0, one launch (start us, length us, event | category | flops | bytes accessed | tf_op | source)
XLA Modules:
  0.0 109.9 jit_solution(1055569576233318482)
XLA Ops:
  1.9 105.4 %band.1 = (bf16[576,1024]{1,0:T(8,128)(2,1)S(1)}, bf16[576,1024]{1,0:T(8,128)(2,1)S(1)}, f32[3]{0:T(128)}) custom-call(bf16[576,1024]{1,0:T(8,128)(2,1)} %bitcast.7, bf16[576,1024]{1,0:T(8,128)(2,1)} %bitcast.8, bf16[8,128]{1,0:T(8,128)(2,1)} %bitcast.9, f32[1]{0:T(128)S(6)} %copy.13.exponent, f32[1]{0:T(128)S(6)} %copy.14.offset), custom_call_target="tpu_custom_call" | custom-call | tf_op jit(solution)/shard_map/band/pallas_call | solution.py:456
  107.3 1.0 copy.11
  108.3 0.0 copy-start
  108.3 1.0 copy.12
  109.3 0.0 copy-done
  109.4 0.5 copy.15
Async XLA Ops:
  108.3 1.0 copy-start

commit v3 on v2

--- a/solution.py
+++ b/solution.py
@@ -18,6 +18,7 @@
 CHUNK = 256
 CHUNKS = SUPER // CHUNK
 AHEAD = 1
+HALVES = 2
 LINE = 8
 LOG2E = math.log2(math.e)
 
@@ -130,12 +131,13 @@
     at_end = jnp.logical_or(left_end, right_end)
     pl.semaphore_wait(barrier, jnp.where(at_end, 4, 3) + (2 * LINE - 1) + (lines - 1))
 
-    def x_copy(a, c):
+    def x_copy(a, c, h):
+        rows = PART // HALVES
         return pltpu.make_async_remote_copy(
-            src_ref=inputs[a].at[:, pl.ds(c * CHUNK, CHUNK)],
-            dst_ref=held.at[a, pl.ds(PART, PART), columns_of(1, c)],
-            send_sem=x_send.at[a, c],
-            recv_sem=x_recv.at[a, c],
+            src_ref=inputs[a].at[pl.ds(h * rows, rows), pl.ds(c * CHUNK, CHUNK)],
+            dst_ref=held.at[a, pl.ds(PART + h * rows, rows), columns_of(1, c)],
+            send_sem=x_send.at[a, c, h],
+            recv_sem=x_recv.at[a, c, h],
             device_id=(sb, away),
             device_id_type=MESH,
         )
@@ -164,7 +166,8 @@
         )
 
     def begin(a, c):
-        x_copy(a, c).start()
+        for h in range(HALVES):
+            x_copy(a, c, h).start()
 
     def begin_sides(a, c):
         for side in range(2):
@@ -248,7 +251,8 @@
 
     def forward(a, c):
         ahead(a, c, begin)
-        x_copy(a, c).wait_recv()
+        for h in range(HALVES):
+            x_copy(a, c, h).wait_recv()
         for side in range(2):
             pl.when(jnp.logical_not(sides[side][2]))(other_copy(a, side, c).start)
         ahead(a, c, begin_sides)
@@ -436,7 +440,8 @@
 
     for a in range(2):
         for c in range(CHUNKS):
-            x_copy(a, c).wait_send()
+            for h in range(HALVES):
+                x_copy(a, c, h).wait_send()
             for side in range(2):
                 own_copy(a, side, c).wait_send()
                 other_copy(a, side, c).wait_send()
@@ -477,8 +482,8 @@
             pltpu.VMEM((8, 128), F32),
             pltpu.VMEM((lines, 8, 128), F32),
             dma((2,)),
-            dma((2, CHUNKS)),
-            dma((2, CHUNKS)),
+            dma((2, CHUNKS, HALVES)),
+            dma((2, CHUNKS, HALVES)),
             dma((2, 2, CHUNKS)),
             dma((2, 2, CHUNKS)),
             dma((2, 2, CHUNKS)),

time: 110 us -> 110 us (level)
  no operation moved by 1% of the time
where the time goes in v3:
time: 110 us
  Pallas kernels  106 us (96%)
  local copies, waits for them, and re-layouts  2.54 us (2%)
  between operations  1.93 us (2%)
    pallas_call x1, Pallas kernels, shards(): pl.pallas_call(functools.partial(kernel, count), out_shape=(pltpu.VMEM((P...  106 us
    unnamed x5, local copies, waits for them, and re-layouts  2.54 us

profile of v3, /device:TPU:0, one launch (start us, length us, event | category | flops | bytes accessed | tf_op | source)
XLA Modules:
  0.0 110.1 jit_solution(11609173867085742489)
XLA Ops:
  1.9 105.6 %band.1 = (bf16[576,1024]{1,0:T(8,128)(2,1)S(1)}, bf16[576,1024]{1,0:T(8,128)(2,1)S(1)}, f32[3]{0:T(128)}) custom-call(bf16[576,1024]{1,0:T(8,128)(2,1)} %bitcast.7, bf16[576,1024]{1,0:T(8,128)(2,1)} %bitcast.8, bf16[8,128]{1,0:T(8,128)(2,1)} %bitcast.9, f32[1]{0:T(128)S(6)} %copy.13.exponent, f32[1]{0:T(128)S(6)} %copy.14.offset), custom_call_target="tpu_custom_call" | custom-call | tf_op jit(solution)/shard_map/band/pallas_call | solution.py:461
  107.5 1.0 copy.11
  108.5 0.0 copy-start
  108.5 1.0 copy.12
  109.5 0.0 copy-done
  109.5 0.5 copy.15
Async XLA Ops:
  108.5 1.0 copy-start
